TPU v7x, 512 devices: a whole 4x8x8 slice. The times are simulated.
512 devices in a mesh: fit: 32 (over y_lo, z), pair: 16 (over x, y_hi, core).
Axes of the slice: x: 4, y: 8 (y_hi: 2, y_lo: 4; y = y_hi * 4 + y_lo), z: 8, core: 2. Of those that a mesh axis runs over, the one named last changes fastest.
Arguments:
- left_factors: bfloat16 [8000, 2048], P('fit'), may hold values from -0.6328125 to 0.6328125
- right_factors: bfloat16 [4, 8000, 2048], P(None, 'fit', 'pair'), may hold values from -0.6328125 to 0.6328125
- virtual_energy: float32 [2048], replicated, may hold values from 0.5 to 3
- internal_energy: float32 [4], replicated, may hold values from -2 to -0.5
- amplitudes: bfloat16 [4, 2048, 2048], P(None, None, 'pair'), may hold values from -0.125 to 0.125
- cfg_map: int32 [4, 8], replicated, may hold values from 0 to 3
- coupling: float32 [4, 8], replicated, may hold values from 0.5 to 2
Outputs:
- residual: bfloat16 [2048, 4, 2048], P('fit', None, 'pair')
All inputs are finite; a program needn't handle non-finite values.
Results may differ from a plain program's by a relative error of at most 0.0044.
Values may be sent and summed in bfloat16 or wider, within the bound.
A program may use at most 64 MiB of HBM per device.

v0:
```python
import jax
import jax.numpy as jnp
from jax import lax
from jax.sharding import PartitionSpec as P


def shards(
    left_factors, right_factors, virtual_energy, internal_energy, amplitudes, cfg_map, coupling
):
    block_rows, width = left_factors.shape
    col_width = right_factors.shape[2]
    row_width = width // lax.axis_size("fit")
    rows = left_factors
    kernel = lax.psum_scatter(
        jnp.einsum("qa,jqc->ajc", rows, right_factors, preferred_element_type=jnp.float32),
        "fit",
        scatter_dimension=0,
        tiled=True,
    )
    row_energy = lax.dynamic_slice_in_dim(
        virtual_energy, lax.axis_index("fit") * row_width, row_width, 0
    )
    col_energy = lax.dynamic_slice_in_dim(
        virtual_energy, lax.axis_index("pair") * col_width, col_width, 0
    )
    denom = row_energy[:, None, None] + col_energy[None, None, :] - internal_energy[None, :, None]
    trial = (kernel / denom).astype(jnp.bfloat16)
    config_count = amplitudes.shape[0]
    picker = (
        cfg_map[:, :, None] == jnp.arange(config_count, dtype=jnp.int32)[None, None, :]
    ).astype(jnp.bfloat16)
    rows = amplitudes
    chosen = jnp.einsum("jnk,kcb->jncb", picker, rows, preferred_element_type=jnp.float32).astype(
        jnp.bfloat16
    )
    inner = jnp.einsum(
        "ajc,jncb->ajnb",
        lax.all_gather(trial, "pair", axis=2, tiled=True),
        chosen,
        preferred_element_type=jnp.float32,
    )
    coupled = jnp.sum(inner * coupling[None, :, :, None], axis=2)
    return (kernel + coupled).astype(jnp.bfloat16)


def solution(mesh):
    placed = (P("fit", None), P(None, "fit", "pair"), P(), P(), P(None, None, "pair"), P(), P())
    return jax.shard_map(
        shards, mesh=mesh, in_specs=placed, out_specs=P("fit", None, "pair"), check_vma=False
    )
```

profile of v0, /device:TPU:1, one launch (start us, length us, event | category | flops | bytes accessed | tf_op | source)
XLA Modules:
  0.0 259.6 jit_solution(11914770047583173286)
XLA Ops:
  6.5 0.0 copy-start
  6.5 0.0 copy-start.3
  6.5 0.0 copy-start.2
  6.5 0.0 reduce-scatter.2.cloned.1.call-start
  6.5 4.1 %fusion.6 = f32[2048,4,128]{2,0,1:T(8,128)} fusion(bf16[250,2048]{1,0:T(8,128)(2,1)} %param.7, bf16[4,250,128]{2,0,1:T(4,128)(2,1)} %param.8), kind=kOutput, calls=%fused_computation.7 | convolution fusion | flops 524288000 | bytes 5474304 | tf_op jit(solution)/shard_map/qa,jqc->ajc/dot_general | solution.py:15
  10.6 0.0 reduce-scatter.2.cloned.1.call-update
  10.7 0.0 all-gather.2.cloned.1.call-start
  10.7 0.8 dynamic_slice.7
  11.5 0.8 dynamic_slice.6
  12.2 0.1 broadcast_add_fusion
  12.3 150.8 %reduce-scatter.2.cloned.1.call-done = f32[64,4,128]{2,0,1:T(8,128)} async-done(((f32[2048,4,128]{2,0,1:T(8,128)}), f32[64,4,128]{2,0,1:T(8,128)}) %reduce-scatter.2.cloned.1.call-update) | async-done | bytes 131088 | tf_op jit(solution)/shard_map/reduce_scatter | solution.py:14
  163.1 0.0 copy-done.3
  163.1 1.6 divide_convert_fusion
  164.7 0.0 all-gather.2.cloned.1.call-update
  164.8 0.0 copy-done
  164.8 0.0 copy-done.2
  164.8 0.0 copy-start.4
  164.8 13.2 %fusion.1 = bf16[4,8,2048,128]{3,1,2,0:T(8,128)(2,1)} fusion(bf16[4,2048,128,1]{2,1,0,3:T(8,128)(2,1)S(1)} %bitcast.18, s32[4,8]{1,0:T(4,128)S(1)} %copy-done.2), kind=kOutput, calls=%fused_computation.2 | convolution fusion | flops 67108992 | bytes 18874496 | tf_op jit(solution)/shard_map/jnk,kcb->jncb/dot_general | solution.py:33
  178.0 0.0 copy-start.1
  178.0 64.9 %all-gather.2.cloned.1.call-done = bf16[64,4,2048]{2,0,1:T(8,128)(2,1)} async-done(((bf16[64,4,128]{2,0,1:T(8,128)(2,1)}), bf16[64,4,2048]{2,0,1:T(8,128)(2,1)}) %all-gather.2.cloned.1.call-update) | async-done | bytes 1048592 | tf_op jit(solution)/shard_map/all_gather | solution.py:38
  242.9 0.0 copy-done.4
  242.9 9.1 %fusion.4 = f32[4,128,64]{1,2,0:T(8,128)S(1)} fusion(bf16[4,8,2048,128]{3,1,2,0:T(8,128)(2,1)} %fusion.1, bf16[64,4,2048]{2,0,1:T(8,128)(2,1)} %all-gather.2.cloned.1.call-done, f32[4,8]{1,0:T(4,128)S(1)} %copy-done.4), kind=kOutput, calls=%fused_computation.5 | convolution fusion | flops 1074233344 | bytes 17956992 | tf_op jit(solution)/shard_map/ajc,jncb->ajnb/dot_general | solution.py:36
  252.1 0.0 copy-done.1
  252.1 0.7 copy.10
  (1 shorter events, 0.0 us)
Async XLA Ops:
  6.5 158.2 %copy-start = (bf16[4,2048,128]{2,1,0:T(8,128)(2,1)S(1)}, bf16[4,2048,128]{2,1,0:T(8,128)(2,1)}, u32[]{:S(2)}) copy-start(bf16[4,2048,128]{2,1,0:T(8,128)(2,1)} %param.11) | copy-start | bytes 6291460
  6.5 156.6 %copy-start.3 = (f32[4]{0:T(128)S(1)}, f32[4]{0:T(128)}, u32[]{:S(2)}) copy-start(f32[4]{0:T(128)} %param.10) | copy-start | bytes 52
  6.5 158.2 %copy-start.2 = (s32[4,8]{1,0:T(4,128)S(1)}, s32[4,8]{1,0:T(4,128)}, u32[]{:S(2)}) copy-start(s32[4,8]{1,0:T(4,128)} %param.12) | copy-start | bytes 388
  6.5 156.6 %reduce-scatter.2.cloned.1.call-start = ((), (), s32[]{:S(2)}) async-start(), calls=%async_computation.1 | async-start | bytes 4325376 | tf_op jit(solution)/shard_map/reduce_scatter | solution.py:14
  10.7 232.3 %all-gather.2.cloned.1.call-start = ((), (), s32[]{:S(2)}) async-start(), calls=%async_computation.2 | async-start | bytes 1114112 | tf_op jit(solution)/shard_map/all_gather | solution.py:38
  164.8 78.1 %copy-start.4 = (f32[4,8]{1,0:T(4,128)S(1)}, f32[4,8]{1,0:T(4,128)}, u32[]{:S(2)}) copy-start(f32[4,8]{1,0:T(4,128)} %param.13) | copy-start | bytes 388
  178.0 74.0 %copy-start.1 = (f32[64,4,128]{2,0,1:T(8,128)S(1)}, f32[64,4,128]{2,0,1:T(8,128)}, u32[]{:S(2)}) copy-start(f32[64,4,128]{2,0,1:T(8,128)} %reduce-scatter.2.cloned.1.call-done) | copy-start | bytes 393220
Sparse Core Ops, SparseCore 0:
  10.8 152.2 reduce-scatter.1
  166.2 76.6 all-gather.1
where the time goes:
time: 260 us
  waiting for transfers between devices  216 us (83%)
  matrix products  26.5 us (10%)
  between operations  13.5 us (5%)
    reduce_scatter x1, waiting for transfers between devices, shards(): lax.psum_scatter(jnp.einsum('qa,jqc->ajc', rows, right_factors, preferred...  151 us
    all_gather x1, waiting for transfers between devices, shards(): lax.all_gather(trial, 'pair', axis=2, tiled=True)  64.9 us
    dot_general x1, matrix products, shards(): jnp.einsum('jnk,kcb->jncb', picker, rows, preferred_element_type=jnp.floa...  13.2 us
    dot_general x1, matrix products, shards(): jnp.einsum('ajc,jncb->ajnb', lax.all_gather(trial, 'pair', axis=2, tiled=...  9.14 us
  transfers between devices with their start and end apart: 2, of which 2 were waited for; matrix products, arithmetic and copies ran while one was open for 6% of the time, Pallas kernels for 0%

commit v1 on v0

v1 whole, which is shorter than its diff:
```python
import functools

import jax
import jax.numpy as jnp
from jax import lax
from jax.experimental import pallas as pl
from jax.experimental.pallas import tpu as pltpu
from jax.sharding import PartitionSpec as P

MESH = pl.DeviceIdType.MESH
NX, NYL, NYH, NZ, NC = 4, 4, 2, 8, 2
NJ, NTERM, NCFG = 4, 8, 4
ROWS, COLS, V, KPAD = 64, 128, 2048, 256
HALF = NZ // 2


def place(x, yh, yl, z, c):
    return (yl * NZ + z, x * (NYH * NC) + yh * NC + c)


def kernel(
    left_ref, right_ref, ve_ref, ie_ref, cfg_ref, cp_ref, amp_hbm, out_ref,
    at, bt, amp, mix, zin, zout, tot, yin, ker, tr,
    amp_sem, zs, zr, ys, yr, hs, hr, xs, xr, cs, cr,
):
    fit, pair = lax.axis_index("fit"), lax.axis_index("pair")
    z, yl = lax.rem(fit, NZ), lax.div(fit, NZ)
    c, yh, x = lax.rem(pair, NC), lax.rem(lax.div(pair, NC), NYH), lax.div(pair, NYH * NC)

    def zdev(k):
        return place(x, yh, yl, lax.rem(z + k + NZ, NZ), c)

    def ydev(k):
        return place(x, yh, lax.rem(yl + k + NYL, NYL), z, c)

    def xdev(k):
        return place(lax.rem(x + k + NX, NX), yh, yl, z, c)

    hdev = place(x, 1 - yh, yl, z, c)
    cdev = place(x, yh, yl, z, 1 - c)

    barrier = pltpu.get_barrier_semaphore()
    partners = [zdev(1), zdev(-1)] + [ydev(k) for k in (1, 2, 3)] + [xdev(k) for k in (1, 2, 3)] + [hdev, cdev]
    for d in partners:
        pl.semaphore_signal(barrier, inc=1, device_id=d, device_id_type=MESH)

    amp_copy = pltpu.make_async_copy(amp_hbm, amp, amp_sem)
    amp_copy.start()

    depth = left_ref.shape[0]
    at[:, :, :, KPAD - 128 :] = jnp.zeros((NYL, NZ, ROWS, 128), jnp.bfloat16)
    bt[:, KPAD - 16 :, :] = jnp.zeros((NJ, 16, COLS), jnp.bfloat16)
    for j in range(NJ):
        bt[j, :depth, :] = right_ref[j]
    for m in range(V // 128):
        piece = left_ref[:, m * 128 : (m + 1) * 128].T
        for s in range(2):
            block = 2 * m + s
            at[block // NZ, block % NZ, :, :depth] = piece[s * ROWS : (s + 1) * ROWS]

    def chunk(owner, j):
        rows = at[:, owner].reshape(NYL * ROWS, KPAD)
        return jnp.dot(rows, bt[j], preferred_element_type=jnp.float32)

    def reach(j, d):
        return HALF if (j + d) % 2 == 0 else HALF - 1

    def owner_at(d, k):
        return lax.rem(z + (k if d == 0 else NZ - k), NZ)

    def zcopy(j, d, h):
        return pltpu.make_async_remote_copy(
            src_ref=zout.at[d, j, h], dst_ref=zin.at[d, j, h],
            send_sem=zs.at[d, j, h], recv_sem=zr.at[d, j, h],
            device_id=zdev(1 if d == 0 else -1), device_id_type=MESH,
        )

    def zsend(j, d, h):
        k = reach(j, d) - h
        value = chunk(owner_at(d, k), j)
        if h > 0:
            zcopy(j, d, h - 1).wait_recv()
            value = value + zin[d, j, h - 1].astype(jnp.float32)
        zout[d, j, h] = value.astype(jnp.bfloat16)
        zcopy(j, d, h).start()

    def ycopy(j, k):
        return pltpu.make_async_remote_copy(
            src_ref=tot.at[j, lax.rem(yl + k, NYL)], dst_ref=yin.at[j, k - 1],
            send_sem=ys.at[j, k - 1], recv_sem=yr.at[j, k - 1],
            device_id=ydev(k), device_id_type=MESH,
        )

    def zlast(j):
        value = chunk(z, j)
        for d in range(2):
            h = reach(j, d) - 1
            zcopy(j, d, h).wait_recv()
            value = value + zin[d, j, h].astype(jnp.float32)
        tot[j] = value.reshape(NYL, ROWS, COLS)
        for k in (1, 2, 3):
            ycopy(j, k).start()

    def slot(px, ph, pc):
        return px * (NYH * NC) + ph * NC + pc

    def tcopy(j, p, send, recv, device):
        return pltpu.make_async_remote_copy(
            src_ref=tr.at[j, p], dst_ref=tr.at[j, p], send_sem=send, recv_sem=recv,
            device_id=device, device_id_type=MESH,
        )

    def hcopy(j):
        return tcopy(j, pair, hs.at[j], hr.at[j], hdev)

    def xcopy(j, far, k):
        return tcopy(j, slot(x, 1 - yh if far else yh, c), xs.at[j, far, k - 1], xr.at[j, far, k - 1], xdev(k))

    def ccopy(j, i):
        if i == 0:
            p = pair
        elif i == 1:
            p = slot(x, 1 - yh, c)
        elif i < 5:
            p = slot(lax.rem(x + NX - (i - 1), NX), yh, c)
        else:
            p = slot(lax.rem(x + NX - (i - 4), NX), 1 - yh, c)
        return tcopy(j, p, cs.at[j, i], cr.at[j, i], cdev)

    row_line = ve_ref[pl.ds(lax.div(fit, 2), 1), :]
    lanes = lax.broadcasted_iota(jnp.int32, (ROWS, 128), 1)
    wanted = lax.broadcasted_iota(jnp.int32, (ROWS, 128), 0) + lax.rem(fit, 2) * ROWS
    row_energy = jnp.sum(jnp.where(lanes == wanted, row_line, 0.0), axis=1, keepdims=True)
    pair_energy = row_energy + ve_ref[pl.ds(pair, 1), :]

    def trial(j):
        value = tot[j, yl]
        for k in (1, 2, 3):
            ycopy(j, k).wait_recv()
            value = value + yin[j, k - 1]
        ker[j] = value
        tr[j, pair] = (value / (pair_energy - ie_ref[j])).astype(jnp.bfloat16)
        hcopy(j).start()
        for k in (1, 2, 3):
            xcopy(j, 0, k).start()
        ccopy(j, 0).start()

    def spread(j):
        hcopy(j).wait_recv()
        for k in (1, 2, 3):
            xcopy(j, 1, k).start()
        ccopy(j, 1).start()
        for k in (1, 2, 3):
            xcopy(j, 0, k).wait_recv()
            ccopy(j, 1 + k).start()

    def swap(j):
        for k in (1, 2, 3):
            xcopy(j, 1, k).wait_recv()
            ccopy(j, 4 + k).start()

    def finish(j):
        for i in range(8):
            ccopy(j, i).wait_recv()
        value = ker[j]
        for q in range(NX * NYH):
            both = jnp.concatenate([tr[j, 2 * q], tr[j, 2 * q + 1]], axis=1)
            value = value + jnp.dot(
                both, mix[j, q * 2 * COLS : (q + 1) * 2 * COLS], preferred_element_type=jnp.float32
            )
        out_ref[j] = value.astype(jnp.bfloat16)

    weight = []
    for j in range(NJ):
        line = []
        for k in range(NCFG):
            total = jnp.float32(0.0)
            for n in range(NTERM):
                total = total + jnp.where(cfg_ref[j, n] == k, cp_ref[j, n], jnp.float32(0.0))
            line.append(total)
        weight.append(line)

    def combine(part):
        rows = slice(part * 256, (part + 1) * 256)
        parts = [amp[k, rows].astype(jnp.float32) for k in range(NCFG)]
        for j in range(NJ):
            value = weight[j][0] * parts[0]
            for k in range(1, NCFG):
                value = value + weight[j][k] * parts[k]
            mix[j, rows] = value.astype(jnp.bfloat16)

    pl.semaphore_wait(barrier, len(partners))
    for j in range(NJ):
        for d in range(2):
            zsend(j, d, 0)
    amp_copy.wait()
    todo = list(range(8))
    for group in ((0, 1), (2, 3)):
        for h in range(1, HALF):
            for j in group:
                for d in range(2):
                    if h < reach(j, d):
                        zsend(j, d, h)
            if todo:
                combine(todo.pop(0))
                combine(todo.pop(0))
            if group == (2, 3):
                if h == 1:
                    trial(0)
                    trial(1)
                elif h == 2:
                    spread(0)
                    spread(1)
                else:
                    swap(0)
                    swap(1)
        for j in group:
            zlast(j)
    while todo:
        combine(todo.pop(0))
    finish(0)
    finish(1)
    for step in (trial, spread, swap, finish):
        for j in (2, 3):
            step(j)

    for j in range(NJ):
        for d in range(2):
            for h in range(reach(j, d)):
                zcopy(j, d, h).wait_send()
        for k in (1, 2, 3):
            ycopy(j, k).wait_send()
            xcopy(j, 0, k).wait_send()
            xcopy(j, 1, k).wait_send()
        hcopy(j).wait_send()
        for i in range(8):
            ccopy(j, i).wait_send()


def shards(left, right, virtual_energy, internal_energy, amplitudes, cfg_map, coupling):
    vmem = pl.BlockSpec(memory_space=pltpu.VMEM)
    smem = pl.BlockSpec(memory_space=pltpu.SMEM)
    dma = pltpu.SemaphoreType.DMA
    out = pl.pallas_call(
        kernel,
        out_shape=jax.ShapeDtypeStruct((NJ, ROWS, COLS), jnp.bfloat16),
        in_specs=[vmem, vmem, vmem, smem, smem, smem, pl.BlockSpec(memory_space=pl.ANY)],
        out_specs=vmem,
        scratch_shapes=[
            pltpu.VMEM((NYL, NZ, ROWS, KPAD), jnp.bfloat16),
            pltpu.VMEM((NJ, KPAD, COLS), jnp.bfloat16),
            pltpu.VMEM((NCFG, V, COLS), jnp.bfloat16),
            pltpu.VMEM((NJ, V, COLS), jnp.bfloat16),
            pltpu.VMEM((2, NJ, HALF, NYL * ROWS, COLS), jnp.bfloat16),
            pltpu.VMEM((2, NJ, HALF, NYL * ROWS, COLS), jnp.bfloat16),
            pltpu.VMEM((NJ, NYL, ROWS, COLS), jnp.float32),
            pltpu.VMEM((NJ, 3, ROWS, COLS), jnp.float32),
            pltpu.VMEM((NJ, ROWS, COLS), jnp.float32),
            pltpu.VMEM((NJ, NX * NYH * NC, ROWS, COLS), jnp.bfloat16),
            dma,
            dma((2, NJ, HALF)),
            dma((2, NJ, HALF)),
            dma((NJ, 3)),
            dma((NJ, 3)),
            dma((NJ,)),
            dma((NJ,)),
            dma((NJ, 2, 3)),
            dma((NJ, 2, 3)),
            dma((NJ, 8)),
            dma((NJ, 8)),
        ],
        compiler_params=pltpu.CompilerParams(
            collective_id=0, has_side_effects=True, vmem_limit_bytes=48 << 20
        ),
        name="exchange",
    )(left, right, virtual_energy.reshape(V // 128, 128), internal_energy, cfg_map, coupling, amplitudes)
    return jnp.transpose(out, (1, 0, 2))


def solution(mesh):
    placed = (P("fit", None), P(None, "fit", "pair"), P(), P(), P(None, None, "pair"), P(), P())
    return jax.shard_map(
        shards, mesh=mesh, in_specs=placed, out_specs=P("fit", None, "pair"), check_vma=False
    )
```

time: 260 us -> 73.2 us (0.28)
  waiting for transfers between devices: 216 us -> 0 us
  Pallas kernels: 0 us -> 65.7 us
  matrix products: 26.5 us -> 0 us
  between operations: 13.5 us -> 0.03 us
  local copies, waits for them, and re-layouts: 2.23 us -> 7.19 us
    reduce_scatter x1 -> x0, waiting for transfers between devices: 151 us -> none  [shards(): lax.psum_scatter(jnp.einsum('qa,jqc->ajc', rows, right_factors, preferred...]
    pallas_call x0 -> x1, Pallas kernels: none -> 65.7 us  [shards(): pl.pallas_call(kernel, out_shape=jax.ShapeDtypeStruct((NJ, ROWS, COLS), j...]
    all_gather x1 -> x0, waiting for transfers between devices: 64.9 us -> none  [shards(): lax.all_gather(trial, 'pair', axis=2, tiled=True)]
    dot_general x3 -> x0, matrix products: 26.5 us -> none  [the longest x1 13.2 us: shards(): jnp.einsum('jnk,kcb->jncb', picker, rows, preferred_element_type=jnp.floa...]
    unnamed x10 -> x13, local copies, waits for them, and re-layouts: 0.02 us -> 6.51 us
  transfers between devices with their start and end apart: 2 -> 0, of which waited for: 2 -> 0; matrix products, arithmetic and copies ran while one was open for 6% -> 0% of each run, Pallas kernels for 0% -> 0%
where the time goes in v1:
time: 73.2 us; the launch traced here: 72.9 us
  Pallas kernels  65.7 us (90%)
  local copies, waits for them, and re-layouts  7.19 us (10%)
    pallas_call x1, Pallas kernels, shards(): pl.pallas_call(kernel, out_shape=jax.ShapeDtypeStruct((NJ, ROWS, COLS), j...  65.7 us
    unnamed x13, local copies, waits for them, and re-layouts  6.51 us

profile of v1, /device:TPU:1, one launch (start us, length us, event | category | flops | bytes accessed | tf_op | source)
XLA Modules:
  0.0 72.9 jit_solution(6707827036584530356)
XLA Ops:
  0.0 1.0 %copy.8.right_ref = bf16[4,250,128]{2,1,0:T(8,128)(2,1)S(1)} copy(bf16[4,250,128]{2,0,1:T(4,128)(2,1)} %param.8) | data formatting | bytes 512000 | tf_op args[1]
  1.0 0.0 copy-start
  1.0 1.6 %copy-done = bf16[4,2048,128]{2,1,0:T(8,128)(2,1)S(1)} copy-done((bf16[4,2048,128]{2,1,0:T(8,128)(2,1)S(1)}, bf16[4,2048,128]{2,1,0:T(8,128)(2,1)}, u32[]{:S(2)}) %copy-start) | copy-done | bytes 2097176
  2.6 0.0 copy-start.1
  2.6 1.2 %copy-done.1 = bf16[250,2048]{1,0:T(8,128)(2,1)S(1)} copy-done((bf16[250,2048]{1,0:T(8,128)(2,1)S(1)}, bf16[250,2048]{1,0:T(8,128)(2,1)}, u32[]{:S(2)}) %copy-start.1) | copy-done | bytes 1024024
  3.8 0.0 copy-start.2
  3.8 0.7 copy-done.2
  4.5 0.0 copy-start.3
  4.5 0.7 copy-done.3
  5.2 0.0 copy-start.4
  5.2 0.7 copy-done.4
  5.9 0.0 copy-start.5
  5.9 0.7 copy-done.5
  6.5 65.7 %exchange.1 = bf16[4,64,128]{2,1,0:T(8,128)(2,1)S(1)} custom-call(bf16[250,2048]{1,0:T(8,128)(2,1)S(1)} %copy-done.1, bf16[4,250,128]{2,1,0:T(8,128)(2,1)S(1)} %copy.8.right_ref, f32[16,128]{1,0:T(8,128)S(1)} %bitcast.3, f32[4]{0:T(128)S(1)} %copy-done.5, s32[4,8]{1,0:T(4,128)S(1)} %copy-done.3, f32[4,8]{1,0:T(4,128)S(1)} %copy-done.4, ...), custom_call_target="tpu_custom_call" | custom-call | tf_op jit(solution)/shard_map/exchange/pallas_call | solution.py:244
  72.2 0.7 copy.9
Async XLA Ops:
  1.0 1.6 %copy-start = (bf16[4,2048,128]{2,1,0:T(8,128)(2,1)S(1)}, bf16[4,2048,128]{2,1,0:T(8,128)(2,1)}, u32[]{:S(2)}) copy-start(bf16[4,2048,128]{2,1,0:T(8,128)(2,1)} %amp_hbm.1) | copy-start | bytes 6291460
  2.6 1.2 %copy-start.1 = (bf16[250,2048]{1,0:T(8,128)(2,1)S(1)}, bf16[250,2048]{1,0:T(8,128)(2,1)}, u32[]{:S(2)}) copy-start(bf16[250,2048]{1,0:T(8,128)(2,1)} %left_ref.1) | copy-start | bytes 3072004
  3.8 0.7 copy-start.2
  4.5 0.7 copy-start.3
  5.2 0.7 copy-start.4
  5.9 0.7 copy-start.5

commit v2 on v0

v2 whole, which is shorter than its diff:
```python
import jax
import jax.numpy as jnp
from jax import lax
from jax.experimental import pallas as pl
from jax.experimental.pallas import tpu as pltpu
from jax.sharding import PartitionSpec as P

MESH = pl.DeviceIdType.MESH
NX, NYL, NYH, NZ, NC = 4, 4, 2, 8, 2
NY = NYL * NYH
NJ, NTERM, NCFG = 4, 8, 4
ROWS, COLS, V, KPAD = 64, 128, 2048, 256
HALF = NZ // 2
GROUPS = ((0, 1), (2, 3))
RING, GATHER = 0, 1
WIDE = 2 * COLS
RELAY = True
ORDER = (
    ('a', 0), ('a', 1), ('b', 0, 0, 0), ('b', 0, 1, 0), ('z', 3, 0, 0), ('z', 3, 1, 0), ('z', 2, 0, 0),
    ('z', 2, 1, 0), ('z', 1, 0, 0), ('z', 1, 1, 0), ('z', 0, 0, 0), ('z', 0, 1, 0), ('b', 1, 0, 0),
    ('b', 1, 1, 0), ('r', 0), ('a', 2), ('z', 3, 0, 1), ('z', 3, 1, 1), ('z', 2, 0, 1), ('z', 2, 1, 1),
    ('z', 1, 0, 1), ('z', 1, 1, 1), ('z', 0, 0, 1), ('z', 0, 1, 1), ('b', 0, 0, 1), ('b', 0, 1, 1),
    ('b', 1, 0, 1), ('b', 1, 1, 1), ('r', 1), ('ax',), ('z', 3, 0, 2), ('z', 3, 1, 2), ('z', 2, 0, 2),
    ('z', 2, 1, 2), ('z', 1, 0, 2), ('z', 1, 1, 2), ('z', 0, 0, 2), ('z', 0, 1, 2), ('b', 0, 0, 2),
    ('b', 0, 1, 2), ('b', 1, 0, 2), ('b', 1, 1, 2), ('r', 2), ('z', 3, 1, 3), ('z', 2, 0, 3), ('z', 1, 1, 3),
    ('z', 0, 0, 3), ('ac',), ('l', 3), ('l', 2), ('l', 1), ('w',), ('l', 0), ('t', 0), ('t', 1), ('s', 0),
    ('s', 1), ('c', 0), ('c', 1), ('f', 0), ('f', 1),
)


def place(x, yh, yl, z, c):
    return (yl * NZ + z, x * (NYH * NC) + yh * NC + c)


def kernel(
    left_hbm, right_hbm, ve_hbm, ie_hbm, cfg_hbm, cp_hbm, amp_hbm, out_ref,
    left_ref, right_ref, ve_ref, ie_ref, cfg_ref, cp_ref, amp, at, bt,
    zin, zout, tot, yin, bin_, ain, csum, cout, cin, ker, tr,
    in_sem, relay, zs, zr, ys, yr, bs, br, as_, ar, axs, axr, acs, acr, ws, wr, hs, hr, xs, xr, cs, cr,
):
    fit, pair = lax.axis_index("fit"), lax.axis_index("pair")
    z, yl = lax.rem(fit, NZ), lax.div(fit, NZ)
    c, yh, x = lax.rem(pair, NC), lax.rem(lax.div(pair, NC), NYH), lax.div(pair, NYH * NC)
    y = yh * NYL + yl

    def zdev(k):
        return place(x, yh, yl, lax.rem(z + k + NZ, NZ), c)

    def ydev(k):
        return place(x, yh, lax.rem(yl + k + NYL, NYL), z, c)

    def around(k):
        other = lax.rem(y + k + NY, NY)
        return place(x, lax.div(other, NYL), lax.rem(other, NYL), z, c)

    def xdev(k):
        return place(lax.rem(x + k + NX, NX), yh, yl, z, c)

    hdev = place(x, 1 - yh, yl, z, c)
    cdev = place(x, yh, yl, z, 1 - c)

    barrier = pltpu.get_barrier_semaphore()
    near = [zdev(1), zdev(-1), around(1), around(-1), xdev(1), xdev(-1)]
    far = [] if RELAY else (
        [zdev(k) for k in range(2, 7)] + [around(k) for k in range(2, 7)] + [xdev(2)]
    )
    for d in near + far + [cdev]:
        pl.semaphore_signal(barrier, inc=1, device_id=d, device_id_type=MESH)

    loads = [
        pltpu.make_async_copy(source, target, in_sem.at[i])
        for i, (source, target) in enumerate(
            [
                (right_hbm, right_ref), (left_hbm, left_ref), (ve_hbm, ve_ref), (ie_hbm, ie_ref),
                (cfg_hbm, cfg_ref), (cp_hbm, cp_ref), (amp_hbm, amp),
            ]
        )
    ]
    for load in loads:
        load.start()

    sent = []

    def start(copy):
        copy.start()
        sent.append(copy)

    def remote(source, target, send, recv, device):
        return pltpu.make_async_remote_copy(
            src_ref=source, dst_ref=target, send_sem=send, recv_sem=recv, device_id=device, device_id_type=MESH
        )

    def greet(r):
        if RELAY:
            for d in near:
                pl.semaphore_signal(relay.at[r], inc=1, device_id=d, device_id_type=MESH)

    def greeted(r):
        if RELAY:
            pl.semaphore_wait(relay.at[r], len(near))
            if r < 2:
                greet(r + 1)

    depth = left_ref.shape[0]
    at[:, :, :, KPAD - 128 :] = jnp.zeros((NYL, NZ, ROWS, 128), jnp.bfloat16)
    bt[:, KPAD - 16 :, :] = jnp.zeros((2, 16, WIDE), jnp.bfloat16)
    loads[0].wait()
    for g, group in enumerate(GROUPS):
        for i, j in enumerate(group):
            bt[g, :depth, i * COLS : (i + 1) * COLS] = right_ref[:, j, :]
    loads[1].wait()
    for m in range(V // 128):
        piece = left_ref[:, m * 128 : (m + 1) * 128].T
        for s in range(2):
            block = 2 * m + s
            at[block // NZ, block % NZ, :, :depth] = piece[s * ROWS : (s + 1) * ROWS]

    def chunk(owner, u):
        return jnp.dot(
            at[lax.rem(yl + u, NYL), owner], bt[RING], preferred_element_type=jnp.float32
        )

    def reach(u, d):
        return HALF if (u + d) % 2 == 0 else HALF - 1

    def owner_at(d, k):
        return lax.rem(z + (k if d == 0 else NZ - k), NZ)

    def zcopy(u, d, h):
        return remote(
            zout.at[d, u, h], zin.at[d, u, h], zs.at[d, u, h], zr.at[d, u, h], zdev(1 if d == 0 else -1)
        )

    def zsend(u, d, h):
        value = chunk(owner_at(d, reach(u, d) - h), u)
        if h > 0:
            zcopy(u, d, h - 1).wait_recv()
            value = value + zin[d, u, h - 1].astype(jnp.float32)
        zout[d, u, h] = value.astype(jnp.bfloat16)
        start(zcopy(u, d, h))

    def ycopy(u):
        return remote(tot.at[u - 1], yin.at[u - 1], ys.at[u - 1], yr.at[u - 1], ydev(u))

    def zlast(u):
        value = chunk(z, u)
        for d in range(2):
            h = reach(u, d) - 1
            zcopy(u, d, h).wait_recv()
            value = value + zin[d, u, h].astype(jnp.float32)
        if u == 0:
            ker[RING] = value
        else:
            tot[u - 1] = value.astype(jnp.bfloat16)
            start(ycopy(u))

    def bcopy(i, d, h):
        part = pl.ds(i * KPAD // 2, KPAD // 2)
        source = bt.at[GATHER, part] if h == 0 else bin_.at[d * 3 + h - 1, part]
        return remote(
            source, bin_.at[d * 3 + h, part], bs.at[d, h, i], br.at[d, h, i], around(1 if d == 0 else -1)
        )

    def bsend(i, d, h):
        if h > 0:
            bcopy(i, d, h - 1).wait_recv()
        start(bcopy(i, d, h))

    def acopy(k):
        step = (1, -1, 2 - 4 * c)[k]
        return remote(
            at.at[lax.rem(yl + step + NYL, NYL), x * NC + c], ain.at[k, x, c], as_.at[k], ar.at[k], around(step)
        )

    def axcopy(k):
        return remote(ain.at[:, x, c], ain.at[:, x, c], axs.at[k - 1], axr.at[k - 1], xdev(k))

    def axsend():
        for k in range(3):
            acopy(k).wait_recv()
        for k in (2, 1, 3):
            start(axcopy(k))

    def accopy():
        return remote(ain.at[:, :, c], ain.at[:, :, c], acs, acr, cdev)

    def acsend():
        for k in (1, 2, 3):
            axcopy(k).wait_recv()
        start(accopy())

    def wcopy(k):
        return remote(cout.at[lax.rem(z + k, NZ)], cin.at[k - 1], ws.at[k - 1], wr.at[k - 1], zdev(k))

    def wsend():
        low, top, mid = 5 * (1 - lax.div(yl + 3, NYL)), 3 - lax.div(yl + 1, NYL), 4 - 3 * lax.div(yl + 2, NYL)
        value = jnp.dot(at[yl].reshape(NZ * ROWS, KPAD), bt[GATHER], preferred_element_type=jnp.float32)
        for i in range(2):
            for d in range(2):
                bcopy(i, d, 2).wait_recv()
        accopy().wait_recv()
        for k, slot_of in enumerate((low, top, mid)):
            value += jnp.dot(ain[k].reshape(NZ * ROWS, KPAD), bin_[slot_of], preferred_element_type=jnp.float32)
        value = value.reshape(NZ, ROWS, WIDE)
        csum[...] = value
        cout[...] = value.astype(jnp.bfloat16)
        for k in (4, 3, 5, 2, 6, 1, 7):
            start(wcopy(k))

    def wjoin():
        value = csum[z]
        for k in (1, 7, 2, 6, 3, 5, 4):
            wcopy(k).wait_recv()
            value = value + cin[k - 1].astype(jnp.float32)
        ker[GATHER] = value

    def yjoin():
        value = ker[RING]
        for k in (1, 2, 3):
            ycopy(k).wait_recv()
            value = value + yin[k - 1].astype(jnp.float32)
        ker[RING] = value

    def hcopy(g):
        mine = tr.at[g, x, yh, c]
        return remote(mine, mine, hs.at[g], hr.at[g], hdev)

    def xcopy(g, other, k):
        mine = tr.at[g, x, 1 - yh if other else yh, c]
        return remote(mine, mine, xs.at[g, other, k - 1], xr.at[g, other, k - 1], xdev(k))

    def ccopy(g, other):
        mine = tr.at[g, :, 1 - yh if other else yh, c]
        return remote(mine, mine, cs.at[g, other], cr.at[g, other], cdev)

    loads[2].wait()
    row_line = ve_ref[pl.ds(lax.div(fit, 2), 1), :]
    lanes = lax.broadcasted_iota(jnp.int32, (ROWS, 128), 1)
    wanted = lax.broadcasted_iota(jnp.int32, (ROWS, 128), 0) + lax.rem(fit, 2) * ROWS
    row_energy = jnp.sum(jnp.where(lanes == wanted, row_line, 0.0), axis=1, keepdims=True)
    pair_energy = row_energy + ve_ref[pl.ds(pair, 1), :]
    for load in loads[3:6]:
        load.wait()
    weight = []
    for j in range(NJ):
        line = []
        for k in range(NCFG):
            total = jnp.float32(0.0)
            for n in range(NTERM):
                total = total + jnp.where(cfg_ref[j, n] == k, cp_ref[j, n], jnp.float32(0.0))
            line.append(total)
        weight.append(line)

    def trial(g):
        (yjoin if g == RING else wjoin)()
        denominator = jnp.concatenate([pair_energy - ie_ref[j] for j in GROUPS[g]], axis=1)
        tr[g, x, yh, c] = (ker[g] / denominator).astype(jnp.bfloat16)
        start(hcopy(g))
        for k in (2, 1, 3):
            start(xcopy(g, 0, k))

    def spread(g):
        hcopy(g).wait_recv()
        for k in (2, 1, 3):
            start(xcopy(g, 1, k))
        for k in (1, 3, 2):
            xcopy(g, 0, k).wait_recv()
        start(ccopy(g, 0))

    def swap(g):
        for k in (1, 3, 2):
            xcopy(g, 1, k).wait_recv()
        start(ccopy(g, 1))

    def finish(g):
        sums = [jnp.zeros((2 * ROWS, WIDE), jnp.float32) for _ in range(NCFG // 2)]
        for other in (0, 1):
            ccopy(g, other).wait_recv()
            for px in range(NX):
                ph = 1 - yh if other else yh
                pieces = [tr[g, px, ph, pc] for pc in range(NC)]
                both = jnp.concatenate(
                    [
                        jnp.concatenate([piece[:, i * COLS : (i + 1) * COLS] for piece in pieces], axis=1)
                        for i in range(2)
                    ],
                    axis=0,
                )
                rows = pl.ds(pl.multiple_of((px * NYH + ph) * WIDE, WIDE), WIDE)
                for k in range(NCFG // 2):
                    pair_of = jnp.concatenate([amp[2 * k, rows], amp[2 * k + 1, rows]], axis=1)
                    sums[k] += jnp.dot(both, pair_of, preferred_element_type=jnp.float32)
        for i, j in enumerate(GROUPS[g]):
            value = ker[g][:, i * COLS : (i + 1) * COLS]
            for k in range(NCFG):
                part = sums[k // 2][i * ROWS : (i + 1) * ROWS, (k % 2) * COLS : (k % 2 + 1) * COLS]
                value = value + weight[j][k] * part
            out_ref[j] = value.astype(jnp.bfloat16)

    pl.semaphore_wait(barrier, len(near + far) + 1)
    greet(0)
    steps = {
        "r": greeted, "z": zsend, "l": zlast, "b": bsend, "a": lambda k: start(acopy(k)), "ax": axsend,
        "ac": acsend, "w": wsend, "t": trial, "s": spread, "c": swap, "f": finish,
    }
    for step in ORDER:
        if step[0] == "f" and loads:
            loads.pop().wait()
            loads.clear()
        steps[step[0]](*step[1:])
    for copy in sent:
        copy.wait_send()


def shards(left, right, virtual_energy, internal_energy, amplitudes, cfg_map, coupling):
    dma = pltpu.SemaphoreType.DMA
    bf16, f32 = jnp.bfloat16, jnp.float32
    out = pl.pallas_call(
        kernel,
        out_shape=pltpu.VMEM((NJ, ROWS, COLS), bf16),
        in_specs=[pl.BlockSpec(memory_space=pl.ANY)] * 7,
        out_specs=pl.BlockSpec(memory_space=pltpu.VMEM),
        scratch_shapes=[
            pltpu.VMEM(left.shape, bf16),
            pltpu.VMEM((left.shape[0], NJ, COLS), bf16),
            pltpu.VMEM((V // 128, 128), f32),
            pltpu.SMEM((NJ,), f32),
            pltpu.SMEM((NJ, NTERM), jnp.int32),
            pltpu.SMEM((NJ, NTERM), f32),
            pltpu.VMEM((NCFG, V, COLS), bf16),
            pltpu.VMEM((NYL, NZ, ROWS, KPAD), bf16),
            pltpu.VMEM((2, KPAD, WIDE), bf16),
            pltpu.VMEM((2, NYL, HALF, ROWS, WIDE), bf16),
            pltpu.VMEM((2, NYL, HALF, ROWS, WIDE), bf16),
            pltpu.VMEM((NYL - 1, ROWS, WIDE), bf16),
            pltpu.VMEM((NYL - 1, ROWS, WIDE), bf16),
            pltpu.VMEM((6, KPAD, WIDE), bf16),
            pltpu.VMEM((3, NX, NC, ROWS, KPAD), bf16),
            pltpu.VMEM((NZ, ROWS, WIDE), f32),
            pltpu.VMEM((NZ, ROWS, WIDE), bf16),
            pltpu.VMEM((NZ - 1, ROWS, WIDE), bf16),
            pltpu.VMEM((2, ROWS, WIDE), f32),
            pltpu.VMEM((2, NX, NYH, NC, ROWS, WIDE), bf16),
            dma((7,)),
            pltpu.SemaphoreType.REGULAR((3,)),
            dma((2, NYL, HALF)),
            dma((2, NYL, HALF)),
            dma((3,)),
            dma((3,)),
            dma((2, 3, 2)),
            dma((2, 3, 2)),
            dma((3,)),
            dma((3,)),
            dma((3,)),
            dma((3,)),
            dma,
            dma,
            dma((NZ - 1,)),
            dma((NZ - 1,)),
            dma((2,)),
            dma((2,)),
            dma((2, 2, 3)),
            dma((2, 2, 3)),
            dma((2, 2)),
            dma((2, 2)),
        ],
        compiler_params=pltpu.CompilerParams(
            collective_id=0, has_side_effects=True, vmem_limit_bytes=56 << 20
        ),
        name="exchange",
    )(left, jnp.transpose(right, (1, 0, 2)), virtual_energy.reshape(V // 128, 128), internal_energy, cfg_map, coupling, amplitudes)
    return jnp.transpose(out, (1, 0, 2))


def solution(mesh):
    placed = (P("fit", None), P(None, "fit", "pair"), P(), P(), P(None, None, "pair"), P(), P())
    return jax.shard_map(
        shards, mesh=mesh, in_specs=placed, out_specs=P("fit", None, "pair"), check_vma=False
    )
```

time: 260 us -> 51.2 us (0.20)
  waiting for transfers between devices: 216 us -> 0 us
  Pallas kernels: 0 us -> 50.4 us
  matrix products: 26.5 us -> 0 us
  between operations: 13.5 us -> 0.01 us
    reduce_scatter x1 -> x0, waiting for transfers between devices: 151 us -> none  [shards(): lax.psum_scatter(jnp.einsum('qa,jqc->ajc', rows, right_factors, preferred...]
    all_gather x1 -> x0, waiting for transfers between devices: 64.9 us -> none  [shards(): lax.all_gather(trial, 'pair', axis=2, tiled=True)]
    pallas_call x0 -> x1, Pallas kernels: none -> 50.4 us  [shards(): pl.pallas_call(kernel, out_shape=pltpu.VMEM((NJ, ROWS, COLS), bf16), in_s...]
    dot_general x3 -> x0, matrix products: 26.5 us -> none  [the longest x1 13.2 us: shards(): jnp.einsum('jnk,kcb->jncb', picker, rows, preferred_element_type=jnp.floa...]
  transfers between devices with their start and end apart: 2 -> 0, of which waited for: 2 -> 0; matrix products, arithmetic and copies ran while one was open for 6% -> 0% of each run, Pallas kernels for 0% -> 0%
where the time goes in v2:
time: 51.2 us; the launch traced here: 51.1 us
  Pallas kernels  50.4 us (98%)
  local copies, waits for them, and re-layouts  0.68 us (1%)
    pallas_call x1, Pallas kernels, shards(): pl.pallas_call(kernel, out_shape=pltpu.VMEM((NJ, ROWS, COLS), bf16), in_s...  50.4 us

profile of v2, /device:TPU:1, one launch (start us, length us, event | category | flops | bytes accessed | tf_op | source)
XLA Modules:
  0.0 51.1 jit_solution(8459355418391205655)
XLA Ops:
  0.0 50.4 %exchange.1 = bf16[4,64,128]{2,1,0:T(8,128)(2,1)S(1)} custom-call(bf16[250,2048]{1,0:T(8,128)(2,1)} %left_hbm.1, bf16[250,4,128]{2,1,0:T(4,128)(2,1)} %bitcast.4, f32[16,128]{1,0:T(8,128)} %bitcast.5, f32[4]{0:T(128)} %ie_hbm.1, s32[4,8]{1,0:T(4,128)} %cfg_hbm.1, f32[4,8]{1,0:T(4,128)} %cp_hbm.1, bf16[4,2048,128]{2,1,0:T(8,128)(2,1)} %amp_hbm.1), custom_call_target="tpu_custom_call" | custom-call | tf_op jit(solution)/shard_map/exchange/pallas_call | solution.py:318
  50.5 0.7 %copy.8 = bf16[64,4,128]{2,1,0:T(4,128)(2,1)} copy(bf16[64,4,128]{2,0,1:T(8,128)(2,1)S(1)} %bitcast.3) | data formatting | bytes 131072 | tf_op jit(solution)/shard_map/transpose | solution.py:372

commit v3 on v2

--- a/solution.py
+++ b/solution.py
@@ -16,15 +16,16 @@
 WIDE = 2 * COLS
 RELAY = True
 ORDER = (
-    ('a', 0), ('a', 1), ('b', 0, 0, 0), ('b', 0, 1, 0), ('z', 3, 0, 0), ('z', 3, 1, 0), ('z', 2, 0, 0),
-    ('z', 2, 1, 0), ('z', 1, 0, 0), ('z', 1, 1, 0), ('z', 0, 0, 0), ('z', 0, 1, 0), ('b', 1, 0, 0),
-    ('b', 1, 1, 0), ('r', 0), ('a', 2), ('z', 3, 0, 1), ('z', 3, 1, 1), ('z', 2, 0, 1), ('z', 2, 1, 1),
-    ('z', 1, 0, 1), ('z', 1, 1, 1), ('z', 0, 0, 1), ('z', 0, 1, 1), ('b', 0, 0, 1), ('b', 0, 1, 1),
-    ('b', 1, 0, 1), ('b', 1, 1, 1), ('r', 1), ('ax',), ('z', 3, 0, 2), ('z', 3, 1, 2), ('z', 2, 0, 2),
-    ('z', 2, 1, 2), ('z', 1, 0, 2), ('z', 1, 1, 2), ('z', 0, 0, 2), ('z', 0, 1, 2), ('b', 0, 0, 2),
-    ('b', 0, 1, 2), ('b', 1, 0, 2), ('b', 1, 1, 2), ('r', 2), ('z', 3, 1, 3), ('z', 2, 0, 3), ('z', 1, 1, 3),
-    ('z', 0, 0, 3), ('ac',), ('l', 3), ('l', 2), ('l', 1), ('w',), ('l', 0), ('t', 0), ('t', 1), ('s', 0),
-    ('s', 1), ('c', 0), ('c', 1), ('f', 0), ('f', 1),
+    ('T',), ('a', 0), ('a', 1), ('b', 0, 0, 0), ('b', 0, 1, 0), ('z', 3, 0, 0), ('z', 3, 1, 0),
+    ('z', 2, 0, 0), ('z', 2, 1, 0), ('z', 1, 0, 0), ('z', 1, 1, 0), ('z', 0, 0, 0), ('z', 0, 1, 0),
+    ('b', 1, 0, 0), ('b', 1, 1, 0), ('r', 0), ('a', 2), ('ax', 0), ('z', 3, 0, 1), ('z', 3, 1, 1),
+    ('z', 2, 0, 1), ('z', 2, 1, 1), ('z', 1, 0, 1), ('z', 1, 1, 1), ('z', 0, 0, 1), ('z', 0, 1, 1),
+    ('b', 0, 0, 1), ('b', 0, 1, 1), ('b', 1, 0, 1), ('b', 1, 1, 1), ('r', 1), ('ax', 1), ('z', 3, 0, 2),
+    ('z', 3, 1, 2), ('z', 2, 0, 2), ('z', 2, 1, 2), ('z', 1, 0, 2), ('z', 1, 1, 2), ('z', 0, 0, 2),
+    ('z', 0, 1, 2), ('ac', 0), ('b', 0, 0, 2), ('b', 0, 1, 2), ('b', 1, 0, 2), ('b', 1, 1, 2), ('r', 2),
+    ('z', 3, 1, 3), ('z', 2, 0, 3), ('z', 1, 1, 3), ('z', 0, 0, 3), ('ac', 1), ('w',), ('l', 3), ('l', 2),
+    ('l', 1), ('l', 0), ('t', 0), ('t', 1), ('s', 0), ('s', 1), ('f', 0, 0), ('c', 0), ('f', 1, 0), ('c', 1),
+    ('f', 0, 1), ('f', 1, 1),
 )
 
 
@@ -76,7 +77,7 @@
             ]
         )
     ]
-    for load in loads:
+    for load in loads[:-1]:
         load.start()
 
     sent = []
@@ -108,12 +109,15 @@
     for g, group in enumerate(GROUPS):
         for i, j in enumerate(group):
             bt[g, :depth, i * COLS : (i + 1) * COLS] = right_ref[:, j, :]
-    loads[1].wait()
-    for m in range(V // 128):
-        piece = left_ref[:, m * 128 : (m + 1) * 128].T
-        for s in range(2):
-            block = 2 * m + s
-            at[block // NZ, block % NZ, :, :depth] = piece[s * ROWS : (s + 1) * ROWS]
+
+    def turn():
+        loads[1].wait()
+        for m in range(V // 128):
+            piece = left_ref[:, m * 128 : (m + 1) * 128].T
+            for s in range(2):
+                block = 2 * m + s
+                at[block // NZ, block % NZ, :, :depth] = piece[s * ROWS : (s + 1) * ROWS]
+        loads[-1].start()
 
     def chunk(owner, u):
         return jnp.dot(
@@ -169,48 +173,70 @@
     def acopy(k):
         step = (1, -1, 2 - 4 * c)[k]
         return remote(
-            at.at[lax.rem(yl + step + NYL, NYL), x * NC + c], ain.at[k, x, c], as_.at[k], ar.at[k], around(step)
-        )
-
-    def axcopy(k):
-        return remote(ain.at[:, x, c], ain.at[:, x, c], axs.at[k - 1], axr.at[k - 1], xdev(k))
-
-    def axsend():
-        for k in range(3):
+            at.at[lax.rem(yl + step + NYL, NYL), c * NX + x], ain.at[k, c, x], as_.at[k], ar.at[k], around(step)
+        )
+
+    batches = ((0, 2), (2, 1))
+
+    def axcopy(part, k):
+        some = ain.at[pl.ds(*batches[part]), c, x]
+        return remote(some, some, axs.at[part, k - 1], axr.at[part, k - 1], xdev(k))
+
+    def axsend(part):
+        first, count = batches[part]
+        for k in range(first, first + count):
             acopy(k).wait_recv()
         for k in (2, 1, 3):
-            start(axcopy(k))
-
-    def accopy():
-        return remote(ain.at[:, :, c], ain.at[:, :, c], acs, acr, cdev)
-
-    def acsend():
-        for k in (1, 2, 3):
-            axcopy(k).wait_recv()
-        start(accopy())
-
-    def wcopy(k):
-        return remote(cout.at[lax.rem(z + k, NZ)], cin.at[k - 1], ws.at[k - 1], wr.at[k - 1], zdev(k))
+            start(axcopy(part, k))
+
+    def accopy(part):
+        some = ain.at[pl.ds(*batches[part]), c]
+        return remote(some, some, acs.at[part], acr.at[part], cdev)
+
+    def acsend(part):
+        for k in (1, 3, 2):
+            axcopy(part, k).wait_recv()
+        start(accopy(part))
+
+    def wcopy(owner):
+        slot_of = lax.rem(owner + NZ - 1 - z, NZ)
+        return remote(
+            cout.at[owner], cin.at[slot_of], ws.at[slot_of], wr.at[slot_of], place(x, yh, yl, owner, c)
+        )
 
     def wsend():
         low, top, mid = 5 * (1 - lax.div(yl + 3, NYL)), 3 - lax.div(yl + 1, NYL), 4 - 3 * lax.div(yl + 2, NYL)
-        value = jnp.dot(at[yl].reshape(NZ * ROWS, KPAD), bt[GATHER], preferred_element_type=jnp.float32)
         for i in range(2):
             for d in range(2):
                 bcopy(i, d, 2).wait_recv()
-        accopy().wait_recv()
-        for k, slot_of in enumerate((low, top, mid)):
-            value += jnp.dot(ain[k].reshape(NZ * ROWS, KPAD), bin_[slot_of], preferred_element_type=jnp.float32)
-        value = value.reshape(NZ, ROWS, WIDE)
-        csum[...] = value
-        cout[...] = value.astype(jnp.bfloat16)
-        for k in (4, 3, 5, 2, 6, 1, 7):
-            start(wcopy(k))
+        for part in range(2):
+            accopy(part).wait_recv()
+        columns = [bt[GATHER]] + [bin_[slot_of] for slot_of in (low, top, mid)]
+        for part in range(2):
+            rows = [at[yl, part * HALF : (part + 1) * HALF]] + [ain[s, part] for s in range(3)]
+            value = sum(
+                jnp.dot(a.reshape(HALF * ROWS, KPAD), b, preferred_element_type=jnp.float32)
+                for a, b in zip(rows, columns)
+            ).reshape(HALF, ROWS, WIDE)
+            csum[part * HALF : (part + 1) * HALF] = value
+            cout[part * HALF : (part + 1) * HALF] = value.astype(jnp.bfloat16)
+            for owner in range(part * HALF, (part + 1) * HALF):
+
+                @pl.when(z != owner)
+                def _():
+                    wcopy(owner).start()
+
+    def wdone():
+        for owner in range(NZ):
+
+            @pl.when(z != owner)
+            def _():
+                wcopy(owner).wait_send()
 
     def wjoin():
         value = csum[z]
         for k in (1, 7, 2, 6, 3, 5, 4):
-            wcopy(k).wait_recv()
+            remote(cout.at[0], cin.at[k - 1], ws.at[k - 1], wr.at[k - 1], zdev(-k)).wait_recv()
             value = value + cin[k - 1].astype(jnp.float32)
         ker[GATHER] = value
 
@@ -222,15 +248,15 @@
         ker[RING] = value
 
     def hcopy(g):
-        mine = tr.at[g, x, yh, c]
+        mine = tr.at[g, yh, c, x]
         return remote(mine, mine, hs.at[g], hr.at[g], hdev)
 
     def xcopy(g, other, k):
-        mine = tr.at[g, x, 1 - yh if other else yh, c]
+        mine = tr.at[g, 1 - yh if other else yh, c, x]
         return remote(mine, mine, xs.at[g, other, k - 1], xr.at[g, other, k - 1], xdev(k))
 
     def ccopy(g, other):
-        mine = tr.at[g, :, 1 - yh if other else yh, c]
+        mine = tr.at[g, 1 - yh if other else yh, c]
         return remote(mine, mine, cs.at[g, other], cr.at[g, other], cdev)
 
     loads[2].wait()
@@ -254,7 +280,7 @@
     def trial(g):
         (yjoin if g == RING else wjoin)()
         denominator = jnp.concatenate([pair_energy - ie_ref[j] for j in GROUPS[g]], axis=1)
-        tr[g, x, yh, c] = (ker[g] / denominator).astype(jnp.bfloat16)
+        tr[g, yh, c, x] = (ker[g] / denominator).astype(jnp.bfloat16)
         start(hcopy(g))
         for k in (2, 1, 3):
             start(xcopy(g, 0, k))
@@ -272,42 +298,46 @@
             xcopy(g, 1, k).wait_recv()
         start(ccopy(g, 1))
 
-    def finish(g):
+    def products(g, other):
+        ccopy(g, other).wait_recv()
         sums = [jnp.zeros((2 * ROWS, WIDE), jnp.float32) for _ in range(NCFG // 2)]
-        for other in (0, 1):
-            ccopy(g, other).wait_recv()
-            for px in range(NX):
-                ph = 1 - yh if other else yh
-                pieces = [tr[g, px, ph, pc] for pc in range(NC)]
-                both = jnp.concatenate(
-                    [
-                        jnp.concatenate([piece[:, i * COLS : (i + 1) * COLS] for piece in pieces], axis=1)
-                        for i in range(2)
-                    ],
-                    axis=0,
-                )
-                rows = pl.ds(pl.multiple_of((px * NYH + ph) * WIDE, WIDE), WIDE)
-                for k in range(NCFG // 2):
-                    pair_of = jnp.concatenate([amp[2 * k, rows], amp[2 * k + 1, rows]], axis=1)
-                    sums[k] += jnp.dot(both, pair_of, preferred_element_type=jnp.float32)
+        ph = 1 - yh if other else yh
+        for px in range(NX):
+            pieces = [tr[g, ph, pc, px] for pc in range(NC)]
+            both = jnp.concatenate(
+                [
+                    jnp.concatenate([piece[:, i * COLS : (i + 1) * COLS] for piece in pieces], axis=1)
+                    for i in range(2)
+                ],
+                axis=0,
+            )
+            rows = pl.ds(pl.multiple_of((px * NYH + ph) * WIDE, WIDE), WIDE)
+            for k in range(NCFG // 2):
+                pair_of = jnp.concatenate([amp[2 * k, rows], amp[2 * k + 1, rows]], axis=1)
+                sums[k] += jnp.dot(both, pair_of, preferred_element_type=jnp.float32)
         for i, j in enumerate(GROUPS[g]):
-            value = ker[g][:, i * COLS : (i + 1) * COLS]
+            cols = slice(i * COLS, (i + 1) * COLS)
+            value = ker[g][:, cols]
             for k in range(NCFG):
                 part = sums[k // 2][i * ROWS : (i + 1) * ROWS, (k % 2) * COLS : (k % 2 + 1) * COLS]
                 value = value + weight[j][k] * part
-            out_ref[j] = value.astype(jnp.bfloat16)
+            if other:
+                out_ref[j] = value.astype(jnp.bfloat16)
+            else:
+                ker[g, :, cols] = value
 
     pl.semaphore_wait(barrier, len(near + far) + 1)
     greet(0)
     steps = {
         "r": greeted, "z": zsend, "l": zlast, "b": bsend, "a": lambda k: start(acopy(k)), "ax": axsend,
-        "ac": acsend, "w": wsend, "t": trial, "s": spread, "c": swap, "f": finish,
+        "ac": acsend, "w": wsend, "t": trial, "s": spread, "c": swap, "f": products, "T": turn,
     }
     for step in ORDER:
         if step[0] == "f" and loads:
             loads.pop().wait()
             loads.clear()
         steps[step[0]](*step[1:])
+    wdone()
     for copy in sent:
         copy.wait_send()
 
@@ -335,12 +365,12 @@
             pltpu.VMEM((NYL - 1, ROWS, WIDE), bf16),
             pltpu.VMEM((NYL - 1, ROWS, WIDE), bf16),
             pltpu.VMEM((6, KPAD, WIDE), bf16),
-            pltpu.VMEM((3, NX, NC, ROWS, KPAD), bf16),
+            pltpu.VMEM((3, NC, NX, ROWS, KPAD), bf16),
             pltpu.VMEM((NZ, ROWS, WIDE), f32),
             pltpu.VMEM((NZ, ROWS, WIDE), bf16),
-            pltpu.VMEM((NZ - 1, ROWS, WIDE), bf16),
+            pltpu.VMEM((NZ, ROWS, WIDE), bf16),
             pltpu.VMEM((2, ROWS, WIDE), f32),
-            pltpu.VMEM((2, NX, NYH, NC, ROWS, WIDE), bf16),
+            pltpu.VMEM((2, NYH, NC, NX, ROWS, WIDE), bf16),
             dma((7,)),
             pltpu.SemaphoreType.REGULAR((3,)),
             dma((2, NYL, HALF)),
@@ -351,12 +381,12 @@
             dma((2, 3, 2)),
             dma((3,)),
             dma((3,)),
-            dma((3,)),
-            dma((3,)),
-            dma,
-            dma,
-            dma((NZ - 1,)),
-            dma((NZ - 1,)),
+            dma((2, 3)),
+            dma((2, 3)),
+            dma((2,)),
+            dma((2,)),
+            dma((NZ,)),
+            dma((NZ,)),
             dma((2,)),
             dma((2,)),
             dma((2, 2, 3)),

time: 51.2 us -> 49.2 us (0.961)
  Pallas kernels: 50.4 us -> 48.4 us
    pallas_call x1, Pallas kernels: 50.4 us -> 48.4 us  [shards(): pl.pallas_call(kernel, out_shape=pltpu.VMEM((NJ, ROWS, COLS), bf16), in_s...]
where the time goes in v3:
time: 49.2 us; the launch traced here: 49.1 us
  Pallas kernels  48.4 us (98%)
  local copies, waits for them, and re-layouts  0.68 us (1%)
    pallas_call x1, Pallas kernels, shards(): pl.pallas_call(kernel, out_shape=pltpu.VMEM((NJ, ROWS, COLS), bf16), in_s...  48.4 us

profile of v3, /device:TPU:1, one launch (start us, length us, event | category | flops | bytes accessed | tf_op | source)
XLA Modules:
  0.0 49.1 jit_solution(2300438958268739944)
XLA Ops:
  0.0 48.4 %exchange.1 = bf16[4,64,128]{2,1,0:T(8,128)(2,1)S(1)} custom-call(bf16[250,2048]{1,0:T(8,128)(2,1)} %left_hbm.1, bf16[250,4,128]{2,1,0:T(4,128)(2,1)} %bitcast.4, f32[16,128]{1,0:T(8,128)} %bitcast.5, f32[4]{0:T(128)} %ie_hbm.1, s32[4,8]{1,0:T(4,128)} %cfg_hbm.1, f32[4,8]{1,0:T(4,128)} %cp_hbm.1, bf16[4,2048,128]{2,1,0:T(8,128)(2,1)} %amp_hbm.1), custom_call_target="tpu_custom_call" | custom-call | tf_op jit(solution)/shard_map/exchange/pallas_call | solution.py:348
  48.4 0.7 %copy.8 = bf16[64,4,128]{2,1,0:T(4,128)(2,1)} copy(bf16[64,4,128]{2,0,1:T(8,128)(2,1)S(1)} %bitcast.3) | data formatting | bytes 131072 | tf_op jit(solution)/shard_map/transpose | solution.py:402

commit v4 on v3

--- a/solution.py
+++ b/solution.py
@@ -16,16 +16,17 @@
 WIDE = 2 * COLS
 RELAY = True
 ORDER = (
-    ('T',), ('a', 0), ('a', 1), ('b', 0, 0, 0), ('b', 0, 1, 0), ('z', 3, 0, 0), ('z', 3, 1, 0),
-    ('z', 2, 0, 0), ('z', 2, 1, 0), ('z', 1, 0, 0), ('z', 1, 1, 0), ('z', 0, 0, 0), ('z', 0, 1, 0),
-    ('b', 1, 0, 0), ('b', 1, 1, 0), ('r', 0), ('a', 2), ('ax', 0), ('z', 3, 0, 1), ('z', 3, 1, 1),
-    ('z', 2, 0, 1), ('z', 2, 1, 1), ('z', 1, 0, 1), ('z', 1, 1, 1), ('z', 0, 0, 1), ('z', 0, 1, 1),
-    ('b', 0, 0, 1), ('b', 0, 1, 1), ('b', 1, 0, 1), ('b', 1, 1, 1), ('r', 1), ('ax', 1), ('z', 3, 0, 2),
-    ('z', 3, 1, 2), ('z', 2, 0, 2), ('z', 2, 1, 2), ('z', 1, 0, 2), ('z', 1, 1, 2), ('z', 0, 0, 2),
-    ('z', 0, 1, 2), ('ac', 0), ('b', 0, 0, 2), ('b', 0, 1, 2), ('b', 1, 0, 2), ('b', 1, 1, 2), ('r', 2),
-    ('z', 3, 1, 3), ('z', 2, 0, 3), ('z', 1, 1, 3), ('z', 0, 0, 3), ('ac', 1), ('w',), ('l', 3), ('l', 2),
-    ('l', 1), ('l', 0), ('t', 0), ('t', 1), ('s', 0), ('s', 1), ('f', 0, 0), ('c', 0), ('f', 1, 0), ('c', 1),
-    ('f', 0, 1), ('f', 1, 1),
+    ('T',), ('a', 0), ('a', 1), ('b', 0, 0, 0), ('b', 0, 1, 0), ('p', 4), ('p', 3), ('p', 5), ('z', 3, 0, 0),
+    ('z', 3, 1, 0), ('z', 2, 0, 0), ('z', 2, 1, 0), ('z', 1, 0, 0), ('z', 1, 1, 0), ('z', 0, 0, 0),
+    ('z', 0, 1, 0), ('b', 1, 0, 0), ('b', 1, 1, 0), ('r', 0), ('a', 2), ('p', 2), ('p', 6), ('p', 1),
+    ('p', 7), ('p', 0), ('ax', 0), ('z', 3, 0, 1), ('z', 3, 1, 1), ('z', 2, 0, 1), ('z', 2, 1, 1),
+    ('z', 1, 0, 1), ('z', 1, 1, 1), ('z', 0, 0, 1), ('z', 0, 1, 1), ('b', 0, 0, 1), ('b', 0, 1, 1),
+    ('b', 1, 0, 1), ('b', 1, 1, 1), ('r', 1), ('ax', 1), ('z', 3, 0, 2), ('z', 3, 1, 2), ('z', 2, 0, 2),
+    ('z', 2, 1, 2), ('z', 1, 0, 2), ('z', 1, 1, 2), ('z', 0, 0, 2), ('z', 0, 1, 2), ('ac', 0), ('b', 0, 0, 2),
+    ('b', 0, 1, 2), ('b', 1, 0, 2), ('b', 1, 1, 2), ('r', 2), ('z', 3, 1, 3), ('z', 2, 0, 3), ('z', 1, 1, 3),
+    ('z', 0, 0, 3), ('ac', 1), ('l', 3), ('w',), ('l', 2), ('l', 1), ('l', 0), ('t', 0), ('t', 1), ('wd',),
+    ('d',), ('s', 0), ('s', 1), ('f', 0, 0), ('c', 0), ('f', 1, 0), ('c', 1), ('d',), ('f', 0, 1),
+    ('f', 1, 1),
 )
 
 
@@ -36,7 +37,7 @@
 def kernel(
     left_hbm, right_hbm, ve_hbm, ie_hbm, cfg_hbm, cp_hbm, amp_hbm, out_ref,
     left_ref, right_ref, ve_ref, ie_ref, cfg_ref, cp_ref, amp, at, bt,
-    zin, zout, tot, yin, bin_, ain, csum, cout, cin, ker, tr,
+    pre, zin, zout, tot, yin, bin_, ain, csum, cout, cin, ker, tr,
     in_sem, relay, zs, zr, ys, yr, bs, br, as_, ar, axs, axr, acs, acr, ws, wr, hs, hr, xs, xr, cs, cr,
 ):
     fit, pair = lax.axis_index("fit"), lax.axis_index("pair")
@@ -119,10 +120,14 @@
                 at[block // NZ, block % NZ, :, :depth] = piece[s * ROWS : (s + 1) * ROWS]
         loads[-1].start()
 
+    def prepare(k):
+        owner = lax.rem(z + k, NZ)
+        rows = at[:, owner].reshape(NYL * ROWS, KPAD)
+        value = jnp.dot(rows, bt[RING], preferred_element_type=jnp.float32)
+        pre[owner] = value.reshape(NYL, ROWS, WIDE)
+
     def chunk(owner, u):
-        return jnp.dot(
-            at[lax.rem(yl + u, NYL), owner], bt[RING], preferred_element_type=jnp.float32
-        )
+        return pre[owner, lax.rem(yl + u, NYL)]
 
     def reach(u, d):
         return HALF if (u + d) % 2 == 0 else HALF - 1
@@ -328,18 +333,21 @@
 
     pl.semaphore_wait(barrier, len(near + far) + 1)
     greet(0)
+    def drain():
+        for copy in sent:
+            copy.wait_send()
+        sent.clear()
+
     steps = {
         "r": greeted, "z": zsend, "l": zlast, "b": bsend, "a": lambda k: start(acopy(k)), "ax": axsend,
-        "ac": acsend, "w": wsend, "t": trial, "s": spread, "c": swap, "f": products, "T": turn,
+        "ac": acsend, "w": wsend, "t": trial, "s": spread, "c": swap, "f": products, "T": turn, "p": prepare, "d": drain, "wd": wdone,
     }
     for step in ORDER:
         if step[0] == "f" and loads:
             loads.pop().wait()
             loads.clear()
         steps[step[0]](*step[1:])
-    wdone()
-    for copy in sent:
-        copy.wait_send()
+    drain()
 
 
 def shards(left, right, virtual_energy, internal_energy, amplitudes, cfg_map, coupling):
@@ -360,6 +368,7 @@
             pltpu.VMEM((NCFG, V, COLS), bf16),
             pltpu.VMEM((NYL, NZ, ROWS, KPAD), bf16),
             pltpu.VMEM((2, KPAD, WIDE), bf16),
+            pltpu.VMEM((NZ, NYL, ROWS, WIDE), f32),
             pltpu.VMEM((2, NYL, HALF, ROWS, WIDE), bf16),
             pltpu.VMEM((2, NYL, HALF, ROWS, WIDE), bf16),
             pltpu.VMEM((NYL - 1, ROWS, WIDE), bf16),

time: 49.2 us -> 48.7 us (0.990)
  Pallas kernels: 48.4 us -> 47.8 us
    pallas_call x1, Pallas kernels: 48.4 us -> 47.8 us  [shards(): pl.pallas_call(kernel, out_shape=pltpu.VMEM((NJ, ROWS, COLS), bf16), in_s...]
where the time goes in v4:
time: 48.7 us; the launch traced here: 48.5 us
  Pallas kernels  47.8 us (98%)
  local copies, waits for them, and re-layouts  0.68 us (1%)
    pallas_call x1, Pallas kernels, shards(): pl.pallas_call(kernel, out_shape=pltpu.VMEM((NJ, ROWS, COLS), bf16), in_s...  47.8 us

profile of v4, /device:TPU:1, one launch (start us, length us, event | category | flops | bytes accessed | tf_op | source)
XLA Modules:
  0.0 48.5 jit_solution(17317380441573326172)
XLA Ops:
  0.0 47.8 %exchange.1 = bf16[4,64,128]{2,1,0:T(8,128)(2,1)S(1)} custom-call(bf16[250,2048]{1,0:T(8,128)(2,1)} %left_hbm.1, bf16[250,4,128]{2,1,0:T(4,128)(2,1)} %bitcast.4, f32[16,128]{1,0:T(8,128)} %bitcast.5, f32[4]{0:T(128)} %ie_hbm.1, s32[4,8]{1,0:T(4,128)} %cfg_hbm.1, f32[4,8]{1,0:T(4,128)} %cp_hbm.1, bf16[4,2048,128]{2,1,0:T(8,128)(2,1)} %amp_hbm.1), custom_call_target="tpu_custom_call" | custom-call | tf_op jit(solution)/shard_map/exchange/pallas_call | solution.py:356
  47.9 0.7 %copy.8 = bf16[64,4,128]{2,1,0:T(4,128)(2,1)} copy(bf16[64,4,128]{2,0,1:T(8,128)(2,1)S(1)} %bitcast.3) | data formatting | bytes 131072 | tf_op jit(solution)/shard_map/transpose | solution.py:411

commit v5 on v4

--- a/solution.py
+++ b/solution.py
@@ -21,12 +21,12 @@
     ('z', 0, 1, 0), ('b', 1, 0, 0), ('b', 1, 1, 0), ('r', 0), ('a', 2), ('p', 2), ('p', 6), ('p', 1),
     ('p', 7), ('p', 0), ('ax', 0), ('z', 3, 0, 1), ('z', 3, 1, 1), ('z', 2, 0, 1), ('z', 2, 1, 1),
     ('z', 1, 0, 1), ('z', 1, 1, 1), ('z', 0, 0, 1), ('z', 0, 1, 1), ('b', 0, 0, 1), ('b', 0, 1, 1),
-    ('b', 1, 0, 1), ('b', 1, 1, 1), ('r', 1), ('ax', 1), ('z', 3, 0, 2), ('z', 3, 1, 2), ('z', 2, 0, 2),
-    ('z', 2, 1, 2), ('z', 1, 0, 2), ('z', 1, 1, 2), ('z', 0, 0, 2), ('z', 0, 1, 2), ('ac', 0), ('b', 0, 0, 2),
-    ('b', 0, 1, 2), ('b', 1, 0, 2), ('b', 1, 1, 2), ('r', 2), ('z', 3, 1, 3), ('z', 2, 0, 3), ('z', 1, 1, 3),
-    ('z', 0, 0, 3), ('ac', 1), ('l', 3), ('w',), ('l', 2), ('l', 1), ('l', 0), ('t', 0), ('t', 1), ('wd',),
-    ('d',), ('s', 0), ('s', 1), ('f', 0, 0), ('c', 0), ('f', 1, 0), ('c', 1), ('d',), ('f', 0, 1),
-    ('f', 1, 1),
+    ('b', 1, 0, 1), ('b', 1, 1, 1), ('m',), ('r', 1), ('ax', 1), ('z', 3, 0, 2), ('z', 3, 1, 2),
+    ('z', 2, 0, 2), ('z', 2, 1, 2), ('z', 1, 0, 2), ('z', 1, 1, 2), ('z', 0, 0, 2), ('z', 0, 1, 2), ('ac', 0),
+    ('b', 0, 0, 2), ('b', 0, 1, 2), ('b', 1, 0, 2), ('b', 1, 1, 2), ('r', 2), ('z', 3, 1, 3), ('z', 2, 0, 3),
+    ('z', 1, 1, 3), ('z', 0, 0, 3), ('ac', 1), ('l', 3), ('w',), ('l', 2), ('l', 1), ('l', 0), ('t', 0),
+    ('t', 1), ('wd',), ('d',), ('s', 0), ('s', 1), ('f', 0, 0), ('c', 0), ('f', 1, 0), ('c', 1), ('d',),
+    ('f', 0, 1), ('f', 1, 1),
 )
 
 
@@ -264,23 +264,27 @@
         mine = tr.at[g, 1 - yh if other else yh, c]
         return remote(mine, mine, cs.at[g, other], cr.at[g, other], cdev)
 
-    loads[2].wait()
-    row_line = ve_ref[pl.ds(lax.div(fit, 2), 1), :]
-    lanes = lax.broadcasted_iota(jnp.int32, (ROWS, 128), 1)
-    wanted = lax.broadcasted_iota(jnp.int32, (ROWS, 128), 0) + lax.rem(fit, 2) * ROWS
-    row_energy = jnp.sum(jnp.where(lanes == wanted, row_line, 0.0), axis=1, keepdims=True)
-    pair_energy = row_energy + ve_ref[pl.ds(pair, 1), :]
-    for load in loads[3:6]:
-        load.wait()
-    weight = []
-    for j in range(NJ):
-        line = []
-        for k in range(NCFG):
-            total = jnp.float32(0.0)
-            for n in range(NTERM):
-                total = total + jnp.where(cfg_ref[j, n] == k, cp_ref[j, n], jnp.float32(0.0))
-            line.append(total)
-        weight.append(line)
+    def settle():
+        nonlocal pair_energy, weight
+        loads[2].wait()
+        row_line = ve_ref[pl.ds(lax.div(fit, 2), 1), :]
+        lanes = lax.broadcasted_iota(jnp.int32, (ROWS, 128), 1)
+        wanted = lax.broadcasted_iota(jnp.int32, (ROWS, 128), 0) + lax.rem(fit, 2) * ROWS
+        row_energy = jnp.sum(jnp.where(lanes == wanted, row_line, 0.0), axis=1, keepdims=True)
+        pair_energy = row_energy + ve_ref[pl.ds(pair, 1), :]
+        for load in loads[3:6]:
+            load.wait()
+        weight = []
+        for j in range(NJ):
+            line = []
+            for k in range(NCFG):
+                total = jnp.float32(0.0)
+                for n in range(NTERM):
+                    total = total + jnp.where(cfg_ref[j, n] == k, cp_ref[j, n], jnp.float32(0.0))
+                line.append(total)
+            weight.append(line)
+
+    pair_energy, weight = None, None
 
     def trial(g):
         (yjoin if g == RING else wjoin)()
@@ -340,7 +344,7 @@
 
     steps = {
         "r": greeted, "z": zsend, "l": zlast, "b": bsend, "a": lambda k: start(acopy(k)), "ax": axsend,
-        "ac": acsend, "w": wsend, "t": trial, "s": spread, "c": swap, "f": products, "T": turn, "p": prepare, "d": drain, "wd": wdone,
+        "ac": acsend, "w": wsend, "t": trial, "s": spread, "c": swap, "f": products, "T": turn, "p": prepare, "d": drain, "wd": wdone, "m": settle,
     }
     for step in ORDER:
         if step[0] == "f" and loads:

time: 48.7 us -> 48.7 us (level)
  no operation moved by 1% of the time
where the time goes in v5:
time: 48.7 us; the launch traced here: 48.6 us
  Pallas kernels  47.9 us (98%)
  local copies, waits for them, and re-layouts  0.68 us (1%)
    pallas_call x1, Pallas kernels, shards(): pl.pallas_call(kernel, out_shape=pltpu.VMEM((NJ, ROWS, COLS), bf16), in_s...  47.9 us

profile of v5, /device:TPU:1, one launch (start us, length us, event | category | flops | bytes accessed | tf_op | source)
XLA Modules:
  0.0 48.6 jit_solution(11730865703953224393)
XLA Ops:
  0.0 47.9 %exchange.1 = bf16[4,64,128]{2,1,0:T(8,128)(2,1)S(1)} custom-call(bf16[250,2048]{1,0:T(8,128)(2,1)} %left_hbm.1, bf16[250,4,128]{2,1,0:T(4,128)(2,1)} %bitcast.4, f32[16,128]{1,0:T(8,128)} %bitcast.5, f32[4]{0:T(128)} %ie_hbm.1, s32[4,8]{1,0:T(4,128)} %cfg_hbm.1, f32[4,8]{1,0:T(4,128)} %cp_hbm.1, bf16[4,2048,128]{2,1,0:T(8,128)(2,1)} %amp_hbm.1), custom_call_target="tpu_custom_call" | custom-call | tf_op jit(solution)/shard_map/exchange/pallas_call | solution.py:360
  47.9 0.7 %copy.8 = bf16[64,4,128]{2,1,0:T(4,128)(2,1)} copy(bf16[64,4,128]{2,0,1:T(8,128)(2,1)S(1)} %bitcast.3) | data formatting | bytes 131072 | tf_op jit(solution)/shard_map/transpose | solution.py:415

commit v6 on v5

--- a/solution.py
+++ b/solution.py
@@ -16,9 +16,9 @@
 WIDE = 2 * COLS
 RELAY = True
 ORDER = (
-    ('T',), ('a', 0), ('a', 1), ('b', 0, 0, 0), ('b', 0, 1, 0), ('p', 4), ('p', 3), ('p', 5), ('z', 3, 0, 0),
-    ('z', 3, 1, 0), ('z', 2, 0, 0), ('z', 2, 1, 0), ('z', 1, 0, 0), ('z', 1, 1, 0), ('z', 0, 0, 0),
-    ('z', 0, 1, 0), ('b', 1, 0, 0), ('b', 1, 1, 0), ('r', 0), ('a', 2), ('p', 2), ('p', 6), ('p', 1),
+    ('T',), ('a', 0), ('a', 1), ('p', 4), ('p', 3), ('p', 5), ('z', 3, 0, 0), ('z', 3, 1, 0), ('z', 2, 0, 0),
+    ('z', 2, 1, 0), ('z', 1, 0, 0), ('z', 1, 1, 0), ('z', 0, 0, 0), ('z', 0, 1, 0), ('b', 0, 0, 0),
+    ('b', 0, 1, 0), ('b', 1, 0, 0), ('b', 1, 1, 0), ('r', 0), ('a', 2), ('p', 2), ('p', 6), ('p', 1),
     ('p', 7), ('p', 0), ('ax', 0), ('z', 3, 0, 1), ('z', 3, 1, 1), ('z', 2, 0, 1), ('z', 2, 1, 1),
     ('z', 1, 0, 1), ('z', 1, 1, 1), ('z', 0, 0, 1), ('z', 0, 1, 1), ('b', 0, 0, 1), ('b', 0, 1, 1),
     ('b', 1, 0, 1), ('b', 1, 1, 1), ('m',), ('r', 1), ('ax', 1), ('z', 3, 0, 2), ('z', 3, 1, 2),

time: 48.7 us -> 48.7 us (level)
  no operation moved by 1% of the time
where the time goes in v6:
time: 48.7 us; the launch traced here: 48.5 us
  Pallas kernels  47.9 us (98%)
  local copies, waits for them, and re-layouts  0.68 us (1%)
    pallas_call x1, Pallas kernels, shards(): pl.pallas_call(kernel, out_shape=pltpu.VMEM((NJ, ROWS, COLS), bf16), in_s...  47.9 us

profile of v6, /device:TPU:1, one launch (start us, length us, event | category | flops | bytes accessed | tf_op | source)
XLA Modules:
  0.0 48.5 jit_solution(16361563588710457477)
XLA Ops:
  0.0 47.9 %exchange.1 = bf16[4,64,128]{2,1,0:T(8,128)(2,1)S(1)} custom-call(bf16[250,2048]{1,0:T(8,128)(2,1)} %left_hbm.1, bf16[250,4,128]{2,1,0:T(4,128)(2,1)} %bitcast.4, f32[16,128]{1,0:T(8,128)} %bitcast.5, f32[4]{0:T(128)} %ie_hbm.1, s32[4,8]{1,0:T(4,128)} %cfg_hbm.1, f32[4,8]{1,0:T(4,128)} %cp_hbm.1, bf16[4,2048,128]{2,1,0:T(8,128)(2,1)} %amp_hbm.1), custom_call_target="tpu_custom_call" | custom-call | tf_op jit(solution)/shard_map/exchange/pallas_call | solution.py:360
  47.9 0.7 %copy.8 = bf16[64,4,128]{2,1,0:T(4,128)(2,1)} copy(bf16[64,4,128]{2,0,1:T(8,128)(2,1)S(1)} %bitcast.3) | data formatting | bytes 131072 | tf_op jit(solution)/shard_map/transpose | solution.py:415
